TPU v7x, 32 devices: a whole 2x2x4 slice. The times are simulated.
32 devices in a mesh: embed: 4 (over x, core), hidden: 8 (over z, y).
Axes of the slice: x: 2, y: 2, z: 4, core: 2. Of those that a mesh axis runs over, the one named last changes fastest.
Arguments:
- rows_in: bfloat16 [128, 16384], P('hidden', 'embed'), may hold values from -6 to 6
- gate_weight: bfloat16 [16384, 28672], P('embed', 'hidden'), may hold values from -0.046875 to 0.046875
- up_weight: bfloat16 [16384, 28672], P('embed', 'hidden'), may hold values from -0.046875 to 0.046875
- down_weight: bfloat16 [28672, 16384], P('hidden', 'embed'), may hold values from -0.03125 to 0.03125
Outputs:
- rows_out: bfloat16 [128, 16384], P('hidden', 'embed')
All inputs are finite; a program needn't handle non-finite values.
Results may differ from a plain program's by a relative error of at most 0.0049.
Values may be sent and summed in bfloat16 or wider, within the bound.
A program may use at most 128 MiB of HBM per device.

v0:
```python
import jax
import jax.numpy as jnp
from jax import lax
from jax.sharding import PartitionSpec as P


def on_device(rows_in, gate_weight, up_weight, down_weight):
    width = gate_weight.shape[1]
    piece = lax.all_gather(rows_in, "hidden", axis=0, tiled=True)
    gate_part = jnp.dot(piece, gate_weight, preferred_element_type=jnp.float32)
    up_part = jnp.dot(piece, up_weight, preferred_element_type=jnp.float32)
    partial_value = jnp.concatenate([gate_part, up_part], axis=1)
    summed = lax.psum(partial_value, "embed")
    activated = (jax.nn.silu(summed[:, :width]) * summed[:, width:]).astype(jnp.bfloat16)
    totals = lax.psum_scatter(
        jnp.dot(activated, down_weight, preferred_element_type=jnp.float32),
        "hidden",
        scatter_dimension=0,
        tiled=True,
    )
    return totals.astype(jnp.bfloat16)


def solution(mesh):
    placed = (
        P("hidden", "embed"),
        P("embed", "hidden"),
        P("embed", "hidden"),
        P("hidden", "embed"),
    )
    return jax.shard_map(
        on_device, mesh=mesh, in_specs=placed, out_specs=P("hidden", "embed"), check_vma=False
    )
```

profile of v0, /device:TPU:0, one launch (start us, length us, event | category | flops | bytes accessed | tf_op | source)
XLA Modules:
  0.0 247.5 jit_solution(6980227807146069996)
XLA Ops:
  6.5 0.0 all-gather.2.cloned.1.call-start
  6.5 0.7 all-gather.2.cloned.1.call-update
  7.3 0.0 all-reduce.2.cloned.1.call-start
  7.3 45.1 %all-gather.2.cloned.1.call-done = bf16[128,4096]{1,0:T(8,128)(2,1)} async-done(((bf16[16,4096]{1,0:T(8,128)(2,1)}), bf16[128,4096]{1,0:T(8,128)(2,1)}) %all-gather.2.cloned.1.call-update) | async-done | bytes 1048592 | tf_op jit(solution)/shard_map/all_gather | solution.py:9
  52.4 0.0 copy-start
  52.4 13.7 %fusion.6 = f32[128,3584]{1,0:T(8,128)S(1)} fusion(bf16[128,4096]{1,0:T(8,128)(2,1)} %all-gather.2.cloned.1.call-done, bf16[4096,3584]{1,0:T(8,128)(2,1)} %param.6), kind=kOutput, calls=%fused_computation.7 | convolution fusion | flops 3758096384 | bytes 32243712 | tf_op jit(solution)/shard_map/dot_general | solution.py:11
  66.1 0.0 copy-done
  66.1 11.5 %fusion.5 = f32[128,3584]{1,0:T(8,128)S(1)} fusion(bf16[128,4096]{1,0:T(8,128)(2,1)S(1)} %copy-done, bf16[4096,3584]{1,0:T(8,128)(2,1)} %param.5), kind=kOutput, calls=%fused_computation.6 | convolution fusion | flops 3758096384 | bytes 32243712 | tf_op jit(solution)/shard_map/dot_general | solution.py:10
  77.6 2.1 pad_maximum_fusion
  79.7 0.0 all-reduce.2.cloned.1.call-update
  79.7 0.0 reduce-scatter.2.cloned.1.call-start
  79.8 75.8 %all-reduce.2.cloned.1.call-done = f32[128,7168]{1,0:T(8,128)} async-done(((f32[128,7168]{1,0:T(8,128)}), f32[128,7168]{1,0:T(8,128)}) %all-reduce.2.cloned.1.call-update) | async-done | bytes 3670032 | tf_op jit(solution)/shard_map/psum | solution.py:13
  155.6 15.9 %fusion.1 = f32[128,4096]{1,0:T(8,128)} fusion(bf16[3584,4096]{1,0:T(8,128)(2,1)} %param.7, f32[128,7168]{1,0:T(8,128)} %all-reduce.2.cloned.1.call-done), kind=kOutput, calls=%fused_computation.3 | convolution fusion | flops 3760848896 | bytes 35127296 | tf_op jit(solution)/shard_map/dot_general | solution.py:16
  171.5 0.0 reduce-scatter.2.cloned.1.call-update
  171.5 67.8 %reduce-scatter.2.cloned.1.call-done = f32[16,4096]{1,0:T(8,128)} async-done(((f32[128,4096]{1,0:T(8,128)}), f32[16,4096]{1,0:T(8,128)}) %reduce-scatter.2.cloned.1.call-update) | async-done | bytes 262160 | tf_op jit(solution)/shard_map/reduce_scatter | solution.py:15
  239.3 1.6 convert_element_type.7
Async XLA Ops:
  6.5 45.8 %all-gather.2.cloned.1.call-start = ((), (), s32[]{:S(2)}) async-start(), calls=%async_computation.1 | async-start | bytes 1179648 | tf_op jit(solution)/shard_map/all_gather | solution.py:9
  7.3 148.3 %all-reduce.2.cloned.1.call-start = ((), (), s32[]{:S(2)}) async-start(), calls=%async_computation.2 | async-start | bytes 7340032 | tf_op jit(solution)/shard_map/psum | solution.py:13
  52.4 13.7 %copy-start = (bf16[128,4096]{1,0:T(8,128)(2,1)S(1)}, bf16[128,4096]{1,0:T(8,128)(2,1)}, u32[]{:S(2)}) copy-start(bf16[128,4096]{1,0:T(8,128)(2,1)} %all-gather.2.cloned.1.call-done) | copy-start | bytes 3145732
  79.7 159.6 %reduce-scatter.2.cloned.1.call-start = ((), (), s32[]{:S(2)}) async-start(), calls=%async_computation.3 | async-start | bytes 2359296 | tf_op jit(solution)/shard_map/reduce_scatter | solution.py:15
Sparse Core Ops, SparseCore 0:
  9.5 42.8 all-gather.1
  79.8 75.7 all-reduce.1
  171.6 67.6 reduce-scatter.1
where the time goes:
time: 248 us; the launch traced here: 247 us
  waiting for transfers between devices  189 us (76%)
  matrix products  41.1 us (17%)
  between operations  13.1 us (5%)
  other arithmetic  3.71 us (1%)
    psum x1, waiting for transfers between devices, on_device(): summed = lax.psum(partial_value, 'embed')  75.8 us
    reduce_scatter x1, waiting for transfers between devices, on_device(): lax.psum_scatter(jnp.dot(activated, down_weight, preferred_element_type=j...  67.8 us
    all_gather x1, waiting for transfers between devices, on_device(): piece = lax.all_gather(rows_in, 'hidden', axis=0, tiled=True)  45.1 us
    dot_general x1, matrix products, on_device(): jnp.dot(activated, down_weight, preferred_element_type=jnp.float32)  15.9 us
    dot_general x1, matrix products, on_device(): up_part = jnp.dot(piece, up_weight, preferred_element_type=jnp.float32)  13.7 us
    dot_general x1, matrix products, on_device(): gate_part = jnp.dot(piece, gate_weight, preferred_element_type=jnp.float32)  11.5 us
  transfers between devices with their start and end apart: 3, of which 3 were waited for; matrix products, arithmetic and copies ran while one was open for 0% of the time, Pallas kernels for 0%

commit v1 on v0

v1 whole, which is shorter than its diff:
```python
import functools

import jax
import jax.numpy as jnp
from jax import lax
from jax.experimental import pallas as pl
from jax.experimental.pallas import tpu as pltpu
from jax.sharding import PartitionSpec as P

MESH = pl.DeviceIdType.MESH
F32 = jnp.float32
BF16 = jnp.bfloat16


def kernel(
    sizes, x_ref, gate_ref, up_ref, down_ref, out_ref,
    xg, wbuf, gu, l1r, l2s, l2r, act, yf, bs, br, zs, zr,
    wsem, own_sem, xa_s, xb_s, x_r, l1_ss, l1_rs, l2_ss, l2_rs,
    ax_ss, ax_rs, ac_ss, ac_rs, b_ss, b_rs, z_ss, z_rs,
):
    X, A, B, C, N, fc, S = sizes
    mine = x_ref.shape[0]
    rows, width = xg.shape
    hidden = act.shape[1]
    half = rows // 2
    rb = half // X
    e, h = lax.axis_index("embed"), lax.axis_index("hidden")
    x, c = e // 2, e % 2
    a, b = h // B, h % B
    half0 = pl.multiple_of(c * half, half)
    other0 = pl.multiple_of((1 - c) * half, half)
    own0 = pl.multiple_of(c * half + x * rb, rb)

    def at_embed(xx, cc):
        return {"embed": xx * 2 + cc, "hidden": h}

    def at_hidden(aa, bb):
        return {"embed": e, "hidden": aa * B + bb}

    def remote(src, dst, send, recv, where):
        return pltpu.make_async_remote_copy(
            src_ref=src, dst_ref=dst, send_sem=send, recv_sem=recv,
            device_id=where, device_id_type=MESH,
        )

    def cols(i):
        return pl.ds(pl.multiple_of(i * fc, fc), fc)

    def gate_tile(i, slot):
        return pltpu.make_async_copy(gate_ref.at[:, cols(i)], wbuf.at[slot, pl.ds(0, width), :], wsem.at[slot])

    def up_tile(i, slot):
        return pltpu.make_async_copy(up_ref.at[:, cols(i)], wbuf.at[slot, pl.ds(0, width), :], wsem.at[slot])

    def down_tile(j, slot):
        return pltpu.make_async_copy(down_ref.at[:, cols(j)], wbuf.at[slot, pl.ds(0, hidden), :], wsem.at[slot])

    for t in range(min(S, 2 * C)):
        (gate_tile if t % 2 == 0 else up_tile)(t // 2, t).start()

    def block(hh):
        return xg.at[pl.ds(pl.multiple_of(hh * mine, mine), mine), :]

    own = pltpu.make_async_copy(x_ref, block(h), own_sem)
    own.start()

    barrier = pltpu.get_barrier_semaphore()
    peers = [at_embed((x + k) % X, c) for k in range(1, X)] + [at_embed(x, 1 - c)]
    peers += [at_hidden((a + k) % A, b) for k in range(1, A)]
    peers += [at_hidden(a, (b + k) % B) for k in range(1, B)]
    for where in peers:
        pl.semaphore_signal(barrier, inc=1, device_id=where, device_id_type=MESH)
    pl.semaphore_wait(barrier, len(peers))

    def x_outer(k):
        return remote(x_ref, block(h), xa_s.at[k], x_r.at[h], at_hidden((a + k) % A, b))

    def x_inner(k, m):
        hh = ((a - k + A) % A) * B + b
        src = x_ref if k == 0 else block(hh)
        return remote(src, block(hh), xb_s.at[k, m], x_r.at[hh], at_hidden(a, (b + m) % B))

    def x_arrived(hh):
        remote(block(hh), block(hh), xa_s.at[0], x_r.at[hh], at_hidden(a, b)).wait_recv()

    for k in range(1, A):
        x_outer(k).start()
    for m in range(1, B):
        x_inner(0, m).start()
    for k in range(1, A):
        x_arrived(((a - k + A) % A) * B + b)
        for m in range(1, B):
            x_inner(k, m).start()
    own.wait()
    for k in range(A):
        for m in range(1, B):
            x_arrived(((a - k + A) % A) * B + (b + m) % B)

    def l1(i):
        return remote(
            gu.at[i, pl.ds(other0, half), :], l1r.at[i], l1_ss.at[i], l1_rs.at[i], at_embed(x, 1 - c))

    def l2(i, k):
        return remote(
            l2s.at[i, k - 1], l2r.at[i, k - 1], l2_ss.at[i, k - 1], l2_rs.at[i, k - 1],
            at_embed((x + k) % X, c))

    def ax(i, k):
        part = act.at[pl.ds(own0, rb), cols(i)]
        return remote(part, part, ax_ss.at[i, k - 1], ax_rs.at[i, k - 1], at_embed((x + k) % X, c))

    def ax_in(i, k):
        xx = (x - k + X) % X
        part = act.at[pl.ds(pl.multiple_of(c * half + xx * rb, rb), rb), cols(i)]
        return remote(part, part, ax_ss.at[i, k - 1], ax_rs.at[i, k - 1], at_embed(x, c))

    def ac(i):
        part = act.at[pl.ds(half0, half), cols(i)]
        return remote(part, part, ac_ss.at[i], ac_rs.at[i], at_embed(x, 1 - c))

    def ac_in(i):
        part = act.at[pl.ds(other0, half), cols(i)]
        return remote(part, part, ac_ss.at[i], ac_rs.at[i], at_embed(x, c))

    def hidden_step(i, _):
        @pl.when(i < C)
        def _():
            s0 = (2 * i) % S
            s1 = s0 + 1
            gate_tile(i, s0).wait()
            gu[i, :, pl.ds(0, fc)] = jnp.dot(
                xg[...], wbuf[s0, pl.ds(0, width), :], preferred_element_type=F32)
            up_tile(i, s1).wait()
            gu[i, :, pl.ds(fc, fc)] = jnp.dot(
                xg[...], wbuf[s1, pl.ds(0, width), :], preferred_element_type=F32)
            l1(i).start()
            t = 2 * i + S

            @pl.when(t < 2 * C)
            def _():
                gate_tile(t // 2, s0).start()
                up_tile(t // 2, s1).start()

            @pl.when((t >= 2 * C) & (t - 2 * C < N))
            def _():
                down_tile(t - 2 * C, s0).start()

            @pl.when((t >= 2 * C) & (t + 1 - 2 * C < N))
            def _():
                down_tile(t + 1 - 2 * C, s1).start()

        @pl.when((i >= 1) & (i < C + 1))
        def _():
            j = i - 1
            l1(j).wait_recv()
            for k in range(1, X):
                xx = (x + k) % X
                there = pl.ds(pl.multiple_of(xx * rb, rb), rb)
                here = pl.ds(pl.multiple_of(c * half + xx * rb, rb), rb)
                l2s[j, k - 1] = (gu[j, here, :] + l1r[j, there, :]).astype(BF16)
                l2(j, k).start()

        @pl.when((i >= 2) & (i < C + 2))
        def _():
            j = i - 2
            total = gu[j, pl.ds(own0, rb), :] + l1r[j, pl.ds(pl.multiple_of(x * rb, rb), rb), :]
            for k in range(1, X):
                l2(j, k).wait_recv()
                total = total + l2r[j, k - 1].astype(F32)
            g, u = total[:, :fc], total[:, fc:]
            act[pl.ds(own0, rb), cols(j)] = (g / (1.0 + jnp.exp(-g)) * u).astype(BF16)
            for k in range(1, X):
                ax(j, k).start()

        @pl.when(i >= 3)
        def _():
            j = i - 3
            for k in range(1, X):
                ax_in(j, k).wait_recv()
            ac(j).start()

        return 0

    lax.fori_loop(0, C + 3, hidden_step, 0)

    def act_in(i, _):
        ac_in(i).wait_recv()
        return 0

    lax.fori_loop(0, C, act_in, 0)

    def sb(j, m):
        return remote(
            bs.at[j, (b + m) % B], br.at[j, m - 1], b_ss.at[j, m - 1], b_rs.at[j, m - 1],
            at_hidden(a, (b + m) % B))

    def sz(j, k):
        return remote(
            zs.at[j, k - 1], zr.at[j, k - 1], z_ss.at[j, k - 1], z_rs.at[j, k - 1],
            at_hidden((a + k) % A, b))

    def inner_sum(j, aa):
        s = yf[j % 3, pl.ds(pl.multiple_of((aa * B + b) * mine, mine), mine), :]
        for m in range(1, B):
            s = s + br[j, m - 1, pl.ds(pl.multiple_of(aa * mine, mine), mine), :].astype(F32)
        return s

    def out_step(i, _):
        @pl.when(i < N)
        def _():
            t = 2 * C + i
            slot = t % S
            down_tile(i, slot).wait()
            yf[i % 3] = jnp.dot(act[...], wbuf[slot, pl.ds(0, hidden), :], preferred_element_type=F32)
            for aa in range(A):
                for bb in range(B):
                    bs[i, bb, pl.ds(aa * mine, mine), :] = yf[
                        i % 3, pl.ds((aa * B + bb) * mine, mine), :].astype(BF16)
            for m in range(1, B):
                sb(i, m).start()

            @pl.when(i + S < N)
            def _():
                down_tile(i + S, slot).start()

        @pl.when((i >= 1) & (i < N + 1))
        def _():
            j = i - 1
            for m in range(1, B):
                sb(j, m).wait_recv()
            for k in range(1, A):
                zs[j, k - 1] = inner_sum(j, (a + k) % A).astype(BF16)
                sz(j, k).start()

        @pl.when(i >= 2)
        def _():
            j = i - 2
            s = inner_sum(j, a)
            for k in range(1, A):
                sz(j, k).wait_recv()
                s = s + zr[j, k - 1].astype(F32)
            out_ref[:, cols(j)] = s.astype(BF16)

        return 0

    lax.fori_loop(0, N + 2, out_step, 0)

    for k in range(1, A):
        x_outer(k).wait_send()
    for k in range(A):
        for m in range(1, B):
            x_inner(k, m).wait_send()

    def hidden_sent(i, _):
        l1(i).wait_send()
        for k in range(1, X):
            l2(i, k).wait_send()
            ax(i, k).wait_send()
        ac(i).wait_send()
        return 0

    lax.fori_loop(0, C, hidden_sent, 0)

    def out_sent(j, _):
        for m in range(1, B):
            sb(j, m).wait_send()
        for k in range(1, A):
            sz(j, k).wait_send()
        return 0

    lax.fori_loop(0, N, out_sent, 0)


def on_device(embed, hidden_size, rows_in, gate_weight, up_weight, down_weight):
    mine, width = rows_in.shape
    hidden = gate_weight.shape[1]
    out_width = down_weight.shape[1]
    rows = mine * hidden_size
    X = embed // 2
    A = 4 if hidden_size % 4 == 0 else 1
    B = hidden_size // A
    C = 7
    fc = hidden // C
    N = out_width // fc
    S = 12
    dma = pltpu.SemaphoreType.DMA
    flops = 2 * rows * hidden * (2 * width + out_width)
    weights = 2 * hidden * (2 * width + out_width)
    half, rb = rows // 2, rows // embed
    return pl.pallas_call(
        functools.partial(kernel, (X, A, B, C, N, fc, S)),
        out_shape=jax.ShapeDtypeStruct((mine, out_width), BF16),
        in_specs=[pl.BlockSpec(memory_space=pl.ANY)] * 4,
        out_specs=pl.BlockSpec(memory_space=pltpu.VMEM),
        scratch_shapes=[
            pltpu.VMEM((rows, width), BF16),
            pltpu.VMEM((S, max(width, hidden), fc), BF16),
            pltpu.VMEM((C, rows, 2 * fc), F32),
            pltpu.VMEM((C, half, 2 * fc), F32),
            pltpu.VMEM((C, X - 1, rb, 2 * fc), BF16),
            pltpu.VMEM((C, X - 1, rb, 2 * fc), BF16),
            pltpu.VMEM((rows, hidden), BF16),
            pltpu.VMEM((3, rows, fc), F32),
            pltpu.VMEM((N, B, A * mine, fc), BF16),
            pltpu.VMEM((N, B - 1, A * mine, fc), BF16),
            pltpu.VMEM((N, A - 1, mine, fc), BF16),
            pltpu.VMEM((N, A - 1, mine, fc), BF16),
            dma((S,)), dma(()), dma((A,)), dma((A, B)), dma((hidden_size,)),
            dma((C,)), dma((C,)), dma((C, X - 1)), dma((C, X - 1)),
            dma((C, X - 1)), dma((C, X - 1)), dma((C,)), dma((C,)),
            dma((N, B - 1)), dma((N, B - 1)), dma((N, A - 1)), dma((N, A - 1)),
        ],
        compiler_params=pltpu.CompilerParams(
            collective_id=0, has_side_effects=True, vmem_limit_bytes=63 * 2**20
        ),
        cost_estimate=pl.CostEstimate(
            flops=flops, bytes_accessed=weights, transcendentals=rows * hidden // embed),
    )(rows_in, gate_weight, up_weight, down_weight)


def solution(mesh):
    placed = (
        P("hidden", "embed"),
        P("embed", "hidden"),
        P("embed", "hidden"),
        P("hidden", "embed"),
    )
    body = functools.partial(on_device, mesh.shape["embed"], mesh.shape["hidden"])
    return jax.shard_map(
        body, mesh=mesh, in_specs=placed, out_specs=P("hidden", "embed"), check_vma=False
    )
```

time: 248 us -> 77.9 us (0.31)
  waiting for transfers between devices: 189 us -> 0 us
  Pallas kernels: 0 us -> 76.2 us
  matrix products: 41.1 us -> 0 us
  between operations: 13.1 us -> 0.01 us
  other arithmetic: 3.71 us -> 0 us
    pallas_call x0 -> x1, Pallas kernels: none -> 76.2 us  [on_device(): pl.pallas_call(functools.partial(kernel, (X, A, B, C, N, fc, S)), out_sha...]
    psum x1 -> x0, waiting for transfers between devices: 75.8 us -> none  [on_device(): summed = lax.psum(partial_value, 'embed')]
    reduce_scatter x1 -> x0, waiting for transfers between devices: 67.8 us -> none  [on_device(): lax.psum_scatter(jnp.dot(activated, down_weight, preferred_element_type=j...]
    all_gather x1 -> x0, waiting for transfers between devices: 45.1 us -> none  [on_device(): piece = lax.all_gather(rows_in, 'hidden', axis=0, tiled=True)]
    dot_general x3 -> x0, matrix products: 41.1 us -> none  [the longest x1 15.9 us: on_device(): jnp.dot(activated, down_weight, preferred_element_type=jnp.float32)]
  transfers between devices with their start and end apart: 3 -> 0, of which waited for: 3 -> 0; matrix products, arithmetic and copies ran while one was open for 0% -> 0% of each run, Pallas kernels for 0% -> 0%
where the time goes in v1:
time: 77.9 us; the launch traced here: 77.8 us
  Pallas kernels  76.2 us (98%)
  local copies, waits for them, and re-layouts  1.57 us (2%)
    pallas_call x1, Pallas kernels, on_device(): pl.pallas_call(functools.partial(kernel, (X, A, B, C, N, fc, S)), out_sha...  76.2 us
    unnamed x1, local copies, waits for them, and re-layouts  1.57 us

profile of v1, /device:TPU:0, one launch (start us, length us, event | category | flops | bytes accessed | tf_op | source)
XLA Modules:
  0.0 77.8 jit_solution(12654492700046002321)
XLA Ops:
  0.0 76.2 %shard_map.46 = bf16[16,4096]{1,0:T(8,128)(2,1)} custom-call(bf16[16,4096]{1,0:T(8,128)(2,1)} %x_ref.1, bf16[4096,3584]{1,0:T(8,128)(2,1)} %gate_ref.1, bf16[4096,3584]{1,0:T(8,128)(2,1)} %up_ref.1, bf16[3584,4096]{1,0:T(8,128)(2,1)} %down_ref.1), custom_call_target="tpu_custom_call" | custom-call | flops 11274289152 | bytes 88080384 | tf_op jit(solution)/shard_map/pallas_call | solution.py:290
  76.2 1.6 %copy.6 = bf16[16,4096]{1,0:T(8,128)(2,1)} copy(bf16[16,4096]{1,0:T(8,128)(2,1)} %shard_map.46) | data formatting | bytes 262144

commit v2 on v1

--- a/solution.py
+++ b/solution.py
@@ -18,7 +18,7 @@
     wsem, own_sem, xa_s, xb_s, x_r, l1_ss, l1_rs, l2_ss, l2_rs,
     ax_ss, ax_rs, ac_ss, ac_rs, b_ss, b_rs, z_ss, z_rs,
 ):
-    X, A, B, C, N, fc, S = sizes
+    X, A, B, C, N, fc, S, G, E, D = sizes
     mine = x_ref.shape[0]
     rows, width = xg.shape
     hidden = act.shape[1]
@@ -72,29 +72,59 @@
         pl.semaphore_signal(barrier, inc=1, device_id=where, device_id_type=MESH)
     pl.semaphore_wait(barrier, len(peers))
 
-    def x_outer(k):
-        return remote(x_ref, block(h), xa_s.at[k], x_r.at[h], at_hidden((a + k) % A, b))
-
-    def x_inner(k, m):
+    part = width // 2
+
+    def piece(ref, q):
+        return ref.at[:, pl.ds(q * part, part)]
+
+    def x_outer(k, q):
+        return remote(
+            piece(x_ref, q), piece(block(h), q), xa_s.at[q, k], x_r.at[q, h], at_hidden((a + k) % A, b))
+
+    def x_inner(k, m, q):
         hh = ((a - k + A) % A) * B + b
-        src = x_ref if k == 0 else block(hh)
-        return remote(src, block(hh), xb_s.at[k, m], x_r.at[hh], at_hidden(a, (b + m) % B))
-
-    def x_arrived(hh):
-        remote(block(hh), block(hh), xa_s.at[0], x_r.at[hh], at_hidden(a, b)).wait_recv()
-
+        src = block(hh) if not isinstance(k, int) or k > 0 else x_ref
+        return remote(
+            piece(src, q), piece(block(hh), q), xb_s.at[q, k, m], x_r.at[q, hh], at_hidden(a, (b + m) % B))
+
+    def x_arrived(hh, q):
+        there = piece(block(hh), q)
+        remote(there, there, xa_s.at[q, 0], x_r.at[q, hh], at_hidden(a, b)).wait_recv()
+
+    def x_forward(k, q):
+        x_arrived(((a - k + A) % A) * B + b, q)
+        for m in range(1, B):
+            x_inner(k, m, q).start()
+
+    def x_rest(q):
+        for k in range(A):
+            for m in range(1, B):
+                x_arrived(((a - k + A) % A) * B + (b + m) % B, q)
+
+    for q in range(2):
+        for k in range(1, A):
+            x_outer(k, q).start()
+        for m in range(1, B):
+            x_inner(0, m, q).start()
     for k in range(1, A):
-        x_outer(k).start()
-    for m in range(1, B):
-        x_inner(0, m).start()
-    for k in range(1, A):
-        x_arrived(((a - k + A) % A) * B + b)
-        for m in range(1, B):
-            x_inner(k, m).start()
+        x_forward(k, 0)
     own.wait()
-    for k in range(A):
-        for m in range(1, B):
-            x_arrived(((a - k + A) % A) * B + (b + m) % B)
+    x_rest(0)
+
+    def early_step(i, _):
+        for n, tile in ((0, gate_tile), (1, up_tile)):
+            tile(i, 2 * i + n).wait()
+            gu[i, :, pl.ds(n * fc, fc)] = jnp.dot(
+                xg[:, pl.ds(0, part)], wbuf[2 * i + n, pl.ds(0, part), :], preferred_element_type=F32)
+
+        @pl.when(i < A - 1)
+        def _():
+            x_forward(i + 1, 1)
+
+        return 0
+
+    lax.fori_loop(0, G, early_step, 0)
+    x_rest(1)
 
     def l1(i):
         return remote(
@@ -123,16 +153,25 @@
         return remote(part, part, ac_ss.at[i], ac_rs.at[i], at_embed(x, c))
 
     def hidden_step(i, _):
+        @pl.when(i < G)
+        def _():
+            for n in range(2):
+                gu[i, :, pl.ds(n * fc, fc)] += jnp.dot(
+                    xg[:, pl.ds(part, part)], wbuf[(2 * i + n) % S, pl.ds(part, part), :],
+                    preferred_element_type=F32)
+
+        @pl.when((i >= G) & (i < C))
+        def _():
+            for n, tile in ((0, gate_tile), (1, up_tile)):
+                slot = (2 * i + n) % S
+                tile(i, slot).wait()
+                gu[i, :, pl.ds(n * fc, fc)] = jnp.dot(
+                    xg[...], wbuf[slot, pl.ds(0, width), :], preferred_element_type=F32)
+
         @pl.when(i < C)
         def _():
             s0 = (2 * i) % S
             s1 = s0 + 1
-            gate_tile(i, s0).wait()
-            gu[i, :, pl.ds(0, fc)] = jnp.dot(
-                xg[...], wbuf[s0, pl.ds(0, width), :], preferred_element_type=F32)
-            up_tile(i, s1).wait()
-            gu[i, :, pl.ds(fc, fc)] = jnp.dot(
-                xg[...], wbuf[s1, pl.ds(0, width), :], preferred_element_type=F32)
             l1(i).start()
             t = 2 * i + S
 
@@ -148,6 +187,20 @@
             @pl.when((t >= 2 * C) & (t + 1 - 2 * C < N))
             def _():
                 down_tile(t + 1 - 2 * C, s1).start()
+
+        @pl.when(i == C)
+        def _():
+            for j in range(E):
+                ac_in(j).wait_recv()
+
+        @pl.when(i >= C)
+        def _():
+            for n in range(D // 3):
+                j = (i - C) * (D // 3) + n
+                slot = (2 * C + j) % S
+                down_tile(j, slot).wait()
+                yf[j] = jnp.dot(
+                    act[:, pl.ds(0, E * fc)], wbuf[slot, pl.ds(0, E * fc), :], preferred_element_type=F32)
 
         @pl.when((i >= 1) & (i < C + 1))
         def _():
@@ -187,7 +240,7 @@
         ac_in(i).wait_recv()
         return 0
 
-    lax.fori_loop(0, C, act_in, 0)
+    lax.fori_loop(E, C, act_in, 0)
 
     def sb(j, m):
         return remote(
@@ -200,22 +253,30 @@
             at_hidden((a + k) % A, b))
 
     def inner_sum(j, aa):
-        s = yf[j % 3, pl.ds(pl.multiple_of((aa * B + b) * mine, mine), mine), :]
+        s = yf[j, pl.ds(pl.multiple_of((aa * B + b) * mine, mine), mine), :]
         for m in range(1, B):
             s = s + br[j, m - 1, pl.ds(pl.multiple_of(aa * mine, mine), mine), :].astype(F32)
         return s
 
     def out_step(i, _):
+        slot = (2 * C + i) % S
+        late = pl.ds(E * fc, hidden - E * fc)
+
+        @pl.when(i < D)
+        def _():
+            yf[i] += jnp.dot(act[:, late], wbuf[slot, late, :], preferred_element_type=F32)
+
+        @pl.when((i >= D) & (i < N))
+        def _():
+            down_tile(i, slot).wait()
+            yf[i] = jnp.dot(act[...], wbuf[slot, pl.ds(0, hidden), :], preferred_element_type=F32)
+
         @pl.when(i < N)
         def _():
-            t = 2 * C + i
-            slot = t % S
-            down_tile(i, slot).wait()
-            yf[i % 3] = jnp.dot(act[...], wbuf[slot, pl.ds(0, hidden), :], preferred_element_type=F32)
             for aa in range(A):
                 for bb in range(B):
                     bs[i, bb, pl.ds(aa * mine, mine), :] = yf[
-                        i % 3, pl.ds((aa * B + bb) * mine, mine), :].astype(BF16)
+                        i, pl.ds((aa * B + bb) * mine, mine), :].astype(BF16)
             for m in range(1, B):
                 sb(i, m).start()
 
@@ -245,11 +306,12 @@
 
     lax.fori_loop(0, N + 2, out_step, 0)
 
-    for k in range(1, A):
-        x_outer(k).wait_send()
-    for k in range(A):
-        for m in range(1, B):
-            x_inner(k, m).wait_send()
+    for q in range(2):
+        for k in range(1, A):
+            x_outer(k, q).wait_send()
+        for k in range(A):
+            for m in range(1, B):
+                x_inner(k, m, q).wait_send()
 
     def hidden_sent(i, _):
         l1(i).wait_send()
@@ -282,13 +344,13 @@
     C = 7
     fc = hidden // C
     N = out_width // fc
-    S = 12
+    S, G, E, D = 12, 4, C - 3, 6
     dma = pltpu.SemaphoreType.DMA
     flops = 2 * rows * hidden * (2 * width + out_width)
     weights = 2 * hidden * (2 * width + out_width)
     half, rb = rows // 2, rows // embed
     return pl.pallas_call(
-        functools.partial(kernel, (X, A, B, C, N, fc, S)),
+        functools.partial(kernel, (X, A, B, C, N, fc, S, G, E, D)),
         out_shape=jax.ShapeDtypeStruct((mine, out_width), BF16),
         in_specs=[pl.BlockSpec(memory_space=pl.ANY)] * 4,
         out_specs=pl.BlockSpec(memory_space=pltpu.VMEM),
@@ -300,12 +362,12 @@
             pltpu.VMEM((C, X - 1, rb, 2 * fc), BF16),
             pltpu.VMEM((C, X - 1, rb, 2 * fc), BF16),
             pltpu.VMEM((rows, hidden), BF16),
-            pltpu.VMEM((3, rows, fc), F32),
+            pltpu.VMEM((N, rows, fc), F32),
             pltpu.VMEM((N, B, A * mine, fc), BF16),
             pltpu.VMEM((N, B - 1, A * mine, fc), BF16),
             pltpu.VMEM((N, A - 1, mine, fc), BF16),
             pltpu.VMEM((N, A - 1, mine, fc), BF16),
-            dma((S,)), dma(()), dma((A,)), dma((A, B)), dma((hidden_size,)),
+            dma((S,)), dma(()), dma((2, A)), dma((2, A, B)), dma((2, hidden_size)),
             dma((C,)), dma((C,)), dma((C, X - 1)), dma((C, X - 1)),
             dma((C, X - 1)), dma((C, X - 1)), dma((C,)), dma((C,)),
             dma((N, B - 1)), dma((N, B - 1)), dma((N, A - 1)), dma((N, A - 1)),

time: 77.9 us -> 80.6 us (1.035)
  Pallas kernels: 76.2 us -> 78.9 us
    pallas_call x1, Pallas kernels: 76.2 us -> 78.9 us  [on_device(): pl.pallas_call(functools.partial(kernel, (X, A, B, C, N, fc, S, G, E, D))...]
where the time goes in v2:
time: 80.6 us; the launch traced here: 80.5 us
  Pallas kernels  78.9 us (98%)
  local copies, waits for them, and re-layouts  1.57 us (2%)
    pallas_call x1, Pallas kernels, on_device(): pl.pallas_call(functools.partial(kernel, (X, A, B, C, N, fc, S, G, E, D))...  78.9 us

profile of v2, /device:TPU:0, one launch (start us, length us, event | category | flops | bytes accessed | tf_op | source)
XLA Modules:
  0.0 80.5 jit_solution(5748355639143343619)
XLA Ops:
  0.0 78.9 %shard_map.46 = bf16[16,4096]{1,0:T(8,128)(2,1)} custom-call(bf16[16,4096]{1,0:T(8,128)(2,1)} %x_ref.1, bf16[4096,3584]{1,0:T(8,128)(2,1)} %gate_ref.1, bf16[4096,3584]{1,0:T(8,128)(2,1)} %up_ref.1, bf16[3584,4096]{1,0:T(8,128)(2,1)} %down_ref.1), custom_call_target="tpu_custom_call" | custom-call | flops 11274289152 | bytes 88080384 | tf_op jit(solution)/shard_map/pallas_call | solution.py:352
  78.9 1.6 %copy.6 = bf16[16,4096]{1,0:T(8,128)(2,1)} copy(bf16[16,4096]{1,0:T(8,128)(2,1)} %shard_map.46) | data formatting | bytes 262144

commit v3 on v2

--- a/solution.py
+++ b/solution.py
@@ -55,8 +55,11 @@
     def down_tile(j, slot):
         return pltpu.make_async_copy(down_ref.at[:, cols(j)], wbuf.at[slot, pl.ds(0, hidden), :], wsem.at[slot])
 
-    for t in range(min(S, 2 * C)):
-        (gate_tile if t % 2 == 0 else up_tile)(t // 2, t).start()
+    def first_tiles(begin, end):
+        for t in range(begin, end):
+            (gate_tile if t % 2 == 0 else up_tile)(t // 2, t).start()
+
+    first_tiles(0, 4)
 
     def block(hh):
         return xg.at[pl.ds(pl.multiple_of(hh * mine, mine), mine), :]
@@ -106,6 +109,7 @@
             x_outer(k, q).start()
         for m in range(1, B):
             x_inner(0, m, q).start()
+    first_tiles(4, S)
     for k in range(1, A):
         x_forward(k, 0)
     own.wait()
@@ -187,20 +191,6 @@
             @pl.when((t >= 2 * C) & (t + 1 - 2 * C < N))
             def _():
                 down_tile(t + 1 - 2 * C, s1).start()
-
-        @pl.when(i == C)
-        def _():
-            for j in range(E):
-                ac_in(j).wait_recv()
-
-        @pl.when(i >= C)
-        def _():
-            for n in range(D // 3):
-                j = (i - C) * (D // 3) + n
-                slot = (2 * C + j) % S
-                down_tile(j, slot).wait()
-                yf[j] = jnp.dot(
-                    act[:, pl.ds(0, E * fc)], wbuf[slot, pl.ds(0, E * fc), :], preferred_element_type=F32)
 
         @pl.when((i >= 1) & (i < C + 1))
         def _():
@@ -232,6 +222,19 @@
                 ax_in(j, k).wait_recv()
             ac(j).start()
 
+        @pl.when(i == C)
+        def _():
+            for j in range(E):
+                ac_in(j).wait_recv()
+
+        @pl.when(i >= C)
+        def _():
+            j = i - C
+            slot = (2 * C + j) % S
+            down_tile(j, slot).wait()
+            yf[j] = jnp.dot(
+                act[:, pl.ds(0, E * fc)], wbuf[slot, pl.ds(0, E * fc), :], preferred_element_type=F32)
+
         return 0
 
     lax.fori_loop(0, C + 3, hidden_step, 0)
@@ -284,18 +287,18 @@
             def _():
                 down_tile(i + S, slot).start()
 
-        @pl.when((i >= 1) & (i < N + 1))
-        def _():
-            j = i - 1
+        @pl.when((i >= 2) & (i < N + 2))
+        def _():
+            j = i - 2
             for m in range(1, B):
                 sb(j, m).wait_recv()
             for k in range(1, A):
                 zs[j, k - 1] = inner_sum(j, (a + k) % A).astype(BF16)
                 sz(j, k).start()
 
-        @pl.when(i >= 2)
-        def _():
-            j = i - 2
+        @pl.when(i >= 4)
+        def _():
+            j = i - 4
             s = inner_sum(j, a)
             for k in range(1, A):
                 sz(j, k).wait_recv()
@@ -304,7 +307,7 @@
 
         return 0
 
-    lax.fori_loop(0, N + 2, out_step, 0)
+    lax.fori_loop(0, N + 4, out_step, 0)
 
     for q in range(2):
         for k in range(1, A):
@@ -344,7 +347,7 @@
     C = 7
     fc = hidden // C
     N = out_width // fc
-    S, G, E, D = 12, 4, C - 3, 6
+    S, G, E, D = 12, 4, C - 3, 3
     dma = pltpu.SemaphoreType.DMA
     flops = 2 * rows * hidden * (2 * width + out_width)
     weights = 2 * hidden * (2 * width + out_width)

time: 80.6 us -> 74.1 us (0.919)
  Pallas kernels: 78.9 us -> 72.4 us
    pallas_call x1, Pallas kernels: 78.9 us -> 72.4 us  [on_device(): pl.pallas_call(functools.partial(kernel, (X, A, B, C, N, fc, S, G, E, D))...]
where the time goes in v3:
time: 74.1 us; the launch traced here: 74 us
  Pallas kernels  72.4 us (98%)
  local copies, waits for them, and re-layouts  1.57 us (2%)
    pallas_call x1, Pallas kernels, on_device(): pl.pallas_call(functools.partial(kernel, (X, A, B, C, N, fc, S, G, E, D))...  72.4 us
    unnamed x1, local copies, waits for them, and re-layouts  1.57 us

profile of v3, /device:TPU:0, one launch (start us, length us, event | category | flops | bytes accessed | tf_op | source)
XLA Modules:
  0.0 74.0 jit_solution(9953631615050688167)
XLA Ops:
  0.0 72.4 %shard_map.46 = bf16[16,4096]{1,0:T(8,128)(2,1)} custom-call(bf16[16,4096]{1,0:T(8,128)(2,1)} %x_ref.1, bf16[4096,3584]{1,0:T(8,128)(2,1)} %gate_ref.1, bf16[4096,3584]{1,0:T(8,128)(2,1)} %up_ref.1, bf16[3584,4096]{1,0:T(8,128)(2,1)} %down_ref.1), custom_call_target="tpu_custom_call" | custom-call | flops 11274289152 | bytes 88080384 | tf_op jit(solution)/shard_map/pallas_call | solution.py:355
  72.4 1.6 %copy.6 = bf16[16,4096]{1,0:T(8,128)(2,1)} copy(bf16[16,4096]{1,0:T(8,128)(2,1)} %shard_map.46) | data formatting | bytes 262144

commit v4 on v3

--- a/solution.py
+++ b/solution.py
@@ -203,9 +203,9 @@
                 l2s[j, k - 1] = (gu[j, here, :] + l1r[j, there, :]).astype(BF16)
                 l2(j, k).start()
 
-        @pl.when((i >= 2) & (i < C + 2))
-        def _():
-            j = i - 2
+        @pl.when((i >= 3) & (i < C + 3))
+        def _():
+            j = i - 3
             total = gu[j, pl.ds(own0, rb), :] + l1r[j, pl.ds(pl.multiple_of(x * rb, rb), rb), :]
             for k in range(1, X):
                 l2(j, k).wait_recv()
@@ -215,21 +215,21 @@
             for k in range(1, X):
                 ax(j, k).start()
 
-        @pl.when(i >= 3)
-        def _():
-            j = i - 3
+        @pl.when(i >= 5)
+        def _():
+            j = i - 5
             for k in range(1, X):
                 ax_in(j, k).wait_recv()
             ac(j).start()
 
-        @pl.when(i == C)
+        @pl.when(i == C + 5 - D)
         def _():
             for j in range(E):
                 ac_in(j).wait_recv()
 
-        @pl.when(i >= C)
-        def _():
-            j = i - C
+        @pl.when(i >= C + 5 - D)
+        def _():
+            j = i - (C + 5 - D)
             slot = (2 * C + j) % S
             down_tile(j, slot).wait()
             yf[j] = jnp.dot(
@@ -237,7 +237,7 @@
 
         return 0
 
-    lax.fori_loop(0, C + 3, hidden_step, 0)
+    lax.fori_loop(0, C + 5, hidden_step, 0)
 
     def act_in(i, _):
         ac_in(i).wait_recv()

time: 74.1 us -> 71.1 us (0.960)
  Pallas kernels: 72.4 us -> 69.4 us
    pallas_call x1, Pallas kernels: 72.4 us -> 69.4 us  [on_device(): pl.pallas_call(functools.partial(kernel, (X, A, B, C, N, fc, S, G, E, D))...]
where the time goes in v4:
time: 71.1 us; the launch traced here: 71 us
  Pallas kernels  69.4 us (98%)
  local copies, waits for them, and re-layouts  1.57 us (2%)
    pallas_call x1, Pallas kernels, on_device(): pl.pallas_call(functools.partial(kernel, (X, A, B, C, N, fc, S, G, E, D))...  69.4 us
    unnamed x1, local copies, waits for them, and re-layouts  1.57 us

profile of v4, /device:TPU:0, one launch (start us, length us, event | category | flops | bytes accessed | tf_op | source)
XLA Modules:
  0.0 71.0 jit_solution(15538766137266620957)
XLA Ops:
  0.0 69.4 %shard_map.46 = bf16[16,4096]{1,0:T(8,128)(2,1)} custom-call(bf16[16,4096]{1,0:T(8,128)(2,1)} %x_ref.1, bf16[4096,3584]{1,0:T(8,128)(2,1)} %gate_ref.1, bf16[4096,3584]{1,0:T(8,128)(2,1)} %up_ref.1, bf16[3584,4096]{1,0:T(8,128)(2,1)} %down_ref.1), custom_call_target="tpu_custom_call" | custom-call | flops 11274289152 | bytes 88080384 | tf_op jit(solution)/shard_map/pallas_call | solution.py:355
  69.4 1.6 %copy.6 = bf16[16,4096]{1,0:T(8,128)(2,1)} copy(bf16[16,4096]{1,0:T(8,128)(2,1)} %shard_map.46) | data formatting | bytes 262144
